TPU v7x, 128 devices: a whole 4x4x4 slice. The times are simulated.
128 devices in a mesh: row: 16 (over z_hi, x, core), col: 8 (over z_lo, y).
Axes of the slice: x: 4, y: 4, z: 4 (z_hi: 2, z_lo: 2; z = z_hi * 2 + z_lo), core: 2. Of those that a mesh axis runs over, the one named last changes fastest.
Arguments:
- doubles: bfloat16 [3600, 3840], P('row', 'col'), may hold values from -6 to 6
- singles: float32 [60, 480], replicated, may hold values from -3 to 3
- integrals: bfloat16 [3840, 32768], P(None, ('col', 'row')), may hold values from -0.09375 to 0.09375
Outputs:
- ladder: bfloat16 [3600, 32768], P('row', 'col')
All inputs are finite; a program needn't handle non-finite values.
Results may differ from a plain program's by a relative error of at most 0.005.
Values may be sent and summed in bfloat16 or wider, within the bound.
A program may use at most 128 MiB of HBM per device.

v0:
```python
import jax
import jax.numpy as jnp
from jax import lax
from jax.sharding import PartitionSpec as P


def onehot_rows(index, count):
    return (index[:, None] == jnp.arange(count, dtype=jnp.int32)[None, :]).astype(jnp.float32)


def build_tau(doubles, singles):
    pair_rows = doubles.shape[0]
    pair_cols = doubles.shape[1]
    occupied = singles.shape[0]
    virtual = singles.shape[1]
    global_row = lax.axis_index("row") * pair_rows + jnp.arange(pair_rows, dtype=jnp.int32)
    global_col = lax.axis_index("col") * pair_cols + jnp.arange(pair_cols, dtype=jnp.int32)
    first_occ = onehot_rows(global_row // occupied, occupied)
    second_occ = onehot_rows(global_row % occupied, occupied)
    first_vir = onehot_rows(global_col // virtual, virtual).T
    second_vir = onehot_rows(global_col % virtual, virtual).T
    exact = lax.Precision.HIGHEST
    left = jnp.dot(jnp.dot(first_occ, singles, precision=exact), first_vir, precision=exact)
    right = jnp.dot(jnp.dot(second_occ, singles, precision=exact), second_vir, precision=exact)
    return (doubles.astype(jnp.float32) + left * right).astype(jnp.bfloat16)


def on_device(doubles, singles, integrals):
    tau_local = build_tau(doubles, singles)
    tau_rows = lax.all_gather(tau_local, "col", axis=1, tiled=True)
    grid_block = lax.all_to_all(integrals, "row", split_axis=0, concat_axis=1, tiled=True)
    summed = jnp.dot(
        tau_rows,
        lax.all_gather(grid_block, "row", axis=0, tiled=True),
        preferred_element_type=jnp.float32,
    )
    return summed.astype(jnp.bfloat16)


def solution(mesh):
    in_specs = (P("row", "col"), P(), P(None, ("col", "row")))
    out_specs = P("row", "col")
    return jax.shard_map(
        on_device, mesh=mesh, in_specs=in_specs, out_specs=out_specs, check_vma=False
    )
```

profile of v0, /device:TPU:1, one launch (start us, length us, event | category | flops | bytes accessed | tf_op | source)
XLA Modules:
  0.0 266.1 jit_solution(14303256013045606890)
XLA Ops:
  6.5 0.0 copy-start
  6.5 0.0 copy-start.2
  6.5 0.0 copy-start.1
  6.5 0.0 all-gather.6.cloned.1.call-start
  6.6 0.8 copy-done
  7.4 0.4 fusion.7
  7.8 0.4 fusion.6
  8.2 0.7 fusion.3
  9.0 0.0 copy-done.2
  9.0 1.5 fusion.2
  10.4 0.0 all-gather.6.cloned.1.call-update
  10.5 0.0 all-gather.4.cloned.1.call-start
  10.5 0.0 copy-done.1
  10.5 51.3 %all_to_all.19 = bf16[16,240,256]{2,1,0:T(8,128)(2,1)S(1)} all-to-all(bf16[16,240,256]{2,1,0:T(8,128)(2,1)S(1)} %bitcast.18), channel_id=1, replica_groups=mesh['row'=16,'col'=8] {'row'}, dimensions={0} | all-to-all | bytes 3932160 | tf_op jit(solution)/shard_map/all_to_all | solution.py:31
  61.8 1.5 copy.8
  63.4 0.0 all-gather.4.cloned.1.call-update
  63.4 0.0 all-gather.6.cloned.1.call-done
  63.4 2.1 copy.6
  65.5 4.2 %reshape.40 = bf16[3840,225]{0,1:T(8,128)(2,1)} reshape(bf16[8,480,225]{1,0,2:T(8,128)(2,1)S(1)} %copy.6) | data formatting | bytes 3456000
  69.7 174.3 %all-gather.4.cloned.1.call-done = bf16[3840,4096]{1,0:T(8,128)(2,1)} async-done(((bf16[240,4096]{1,0:T(8,128)(2,1)}), bf16[3840,4096]{1,0:T(8,128)(2,1)}) %all-gather.4.cloned.1.call-update) | async-done | bytes 31457296 | tf_op jit(solution)/shard_map/all_gather | solution.py:34
  244.1 15.2 %convolution_convert_fusion = bf16[225,4096]{1,0:T(8,128)(2,1)} fusion(bf16[3840,225]{0,1:T(8,128)(2,1)} %reshape.40, bf16[3840,4096]{1,0:T(8,128)(2,1)} %all-gather.4.cloned.1.call-done), kind=kOutput, calls=%fused_computation | convolution fusion | flops 7078809600 | bytes 35028480 | tf_op jit(solution)/shard_map/dot_general | solution.py:32
  (2 shorter events, 0.0 us)
Async XLA Ops:
  6.5 0.9 copy-start
  6.5 2.4 copy-start.2
  6.5 4.0 %copy-start.1 = (bf16[3840,256]{1,0:T(8,128)(2,1)S(1)}, bf16[3840,256]{1,0:T(8,128)(2,1)}, u32[]{:S(2)}) copy-start(bf16[3840,256]{1,0:T(8,128)(2,1)} %param.5) | copy-start | bytes 5898244
  6.5 56.9 %all-gather.6.cloned.1.call-start = ((), (), s32[]{:S(2)}) async-start(), calls=%async_computation.2 | async-start | bytes 2138112 | tf_op jit(solution)/shard_map/all_gather | solution.py:30
  10.5 233.6 %all-gather.4.cloned.1.call-start = ((), (), s32[]{:S(2)}) async-start(), calls=%async_computation.1 | async-start | bytes 33423360 | tf_op jit(solution)/shard_map/all_gather | solution.py:34
Sparse Core Ops, SparseCore 0:
  10.6 48.8 all-gather.5
  63.5 180.5 all-gather.3
where the time goes:
time: 266 us
  waiting for transfers between devices  174 us (65%)
  blocking collectives  51.3 us (19%)
  matrix products  18.2 us (7%)
  between operations  13.5 us (5%)
  local copies, waits for them, and re-layouts  8.71 us (3%)
    all_gather x1, waiting for transfers between devices, on_device(): lax.all_gather(grid_block, 'row', axis=0, tiled=True)  174 us
    all_to_all x1, blocking collectives, on_device(): lax.all_to_all(integrals, 'row', split_axis=0, concat_axis=1, tiled=True)  51.3 us
    dot_general x1, matrix products, on_device(): jnp.dot(tau_rows, lax.all_gather(grid_block, 'row', axis=0, tiled=True),...  15.2 us
  transfers between devices with their start and end apart: 2, of which 1 were waited for; matrix products, arithmetic and copies ran while one was open for 3% of the time, Pallas kernels for 0%

commit v1 on v0

--- a/solution.py
+++ b/solution.py
@@ -31,7 +31,9 @@
     grid_block = lax.all_to_all(integrals, "row", split_axis=0, concat_axis=1, tiled=True)
     summed = jnp.dot(
         tau_rows,
-        lax.all_gather(grid_block, "row", axis=0, tiled=True),
+        jnp.concatenate(
+            lax.all_to_all(jnp.stack([grid_block] * lax.axis_size("row")), "row", 0, 0), axis=0
+        ),
         preferred_element_type=jnp.float32,
     )
     return summed.astype(jnp.bfloat16)

time: 266 us -> 525 us (1.97)
  waiting for transfers between devices: 174 us -> 433 us
  blocking collectives: 51.3 us -> 35.9 us
  local copies, waits for them, and re-layouts: 8.71 us -> 17.2 us
  starting transfers between devices: 0.04 us -> 6.66 us
    all_to_all x0 -> x1, waiting for transfers between devices: none -> 380 us  [on_device(): lax.all_to_all(jnp.stack([grid_block] * lax.axis_size('row')), 'row', 0, 0)]
    all_gather x1 -> x0, waiting for transfers between devices: 174 us -> none  [on_device(): lax.all_gather(grid_block, 'row', axis=0, tiled=True)]
    all_gather x1, waiting for transfers between devices: 0.02 us -> 53.4 us  [on_device(): tau_rows = lax.all_gather(tau_local, 'col', axis=1, tiled=True)]
    all_to_all x1, blocking collectives: 51.3 us -> 35.9 us  [on_device(): lax.all_to_all(integrals, 'row', split_axis=0, concat_axis=1, tiled=True)]
    another operation x0 -> x2, local copies, waits for them, and re-layouts: none -> 10.8 us  [on_device(): jnp.stack([grid_block] * lax.axis_size('row'))]
    all_to_all x0 -> x1, starting transfers between devices: none -> 6.62 us  [on_device(): lax.all_to_all(jnp.stack([grid_block] * lax.axis_size('row')), 'row', 0, 0)]
  transfers between devices with their start and end apart: 2 -> 2, of which waited for: 1 -> 2; matrix products, arithmetic and copies ran while one was open for 3% -> 2% of each run, Pallas kernels for 0% -> 0%
where the time goes in v1:
time: 525 us
  waiting for transfers between devices  433 us (82%)
  blocking collectives  35.9 us (7%)
  matrix products  18.2 us (3%)
  local copies, waits for them, and re-layouts  17.2 us (3%)
  between operations  13.5 us (3%)
  starting transfers between devices  6.66 us (1%)
    all_to_all x1, waiting for transfers between devices, on_device(): lax.all_to_all(jnp.stack([grid_block] * lax.axis_size('row')), 'row', 0, 0)  380 us
    all_gather x1, waiting for transfers between devices, on_device(): tau_rows = lax.all_gather(tau_local, 'col', axis=1, tiled=True)  53.4 us
    all_to_all x1, blocking collectives, on_device(): lax.all_to_all(integrals, 'row', split_axis=0, concat_axis=1, tiled=True)  35.9 us
    dot_general x1, matrix products, on_device(): jnp.dot(tau_rows, jnp.concatenate(lax.all_to_all(jnp.stack([grid_block] *...  15.2 us
    another operation x2, local copies, waits for them, and re-layouts, on_device(): jnp.stack([grid_block] * lax.axis_size('row'))  10.8 us
  transfers between devices with their start and end apart: 2, of which 2 were waited for; matrix products, arithmetic and copies ran while one was open for 2% of the time, Pallas kernels for 0%

profile of v1, /device:TPU:1, one launch (start us, length us, event | category | flops | bytes accessed | tf_op | source)
XLA Modules:
  0.0 524.8 jit_solution(15253239911508701301)
XLA Ops:
  6.5 0.0 copy-start
  6.5 35.9 %all_to_all.21 = bf16[16,240,256]{2,1,0:T(8,128)(2,1)S(1)} all-to-all(bf16[16,240,256]{2,1,0:T(8,128)(2,1)} %bitcast.19), channel_id=1, replica_groups=mesh['row'=16,'col'=8] {'row'}, dimensions={0} | all-to-all | bytes 3932160 | tf_op jit(solution)/shard_map/all_to_all | solution.py:31
  42.4 0.2 copy.8
  42.7 10.6 %stack.5 = bf16[16,240,4096]{2,1,0:T(8,128)(2,1)} broadcast(bf16[240,4096]{1,0:T(8,128)(2,1)S(1)} %bitcast.17), dimensions={1,2} | broadcast | bytes 33423360 | tf_op jit(solution)/shard_map/stack | solution.py:35
  53.3 6.6 %all-to-all-start.1 = ((bf16[16,240,4096]{2,1,0:T(8,128)(2,1)}), bf16[16,240,4096]{2,1,0:T(8,128)(2,1)}, u32[]{:S(2)}, u32[]{:S(2)}) async-start(bf16[16,240,4096]{2,1,0:T(8,128)(2,1)} %stack.5), calls=%async_computation.1 | async-start | bytes 62914560 | tf_op jit(solution)/shard_map/all_to_all | solution.py:35
  59.9 0.0 copy-start.1
  59.9 0.0 all-gather.3.cloned.1.call-start
  60.0 0.0 copy-done
  60.0 0.4 fusion.7
  60.4 0.4 fusion.6
  60.8 0.7 fusion.3
  61.5 0.0 copy-done.1
  61.5 1.4 fusion.2
  63.0 0.0 all-gather.3.cloned.1.call-update
  63.0 53.4 %all-gather.3.cloned.1.call-done = bf16[8,480,225]{1,2,0:T(8,128)(2,1)} async-done(((bf16[1,480,225]{1,2,0:T(8,128)(2,1)}), bf16[8,480,225]{1,2,0:T(8,128)(2,1)}) %all-gather.3.cloned.1.call-update) | async-done | bytes 1728016 | tf_op jit(solution)/shard_map/all_gather | solution.py:30
  116.5 2.1 copy.6
  118.6 4.3 reshape.47
  122.8 379.9 %all-to-all-done.1 = bf16[16,240,4096]{2,1,0:T(8,128)(2,1)} async-done(((bf16[16,240,4096]{2,1,0:T(8,128)(2,1)}), bf16[16,240,4096]{2,1,0:T(8,128)(2,1)}, u32[]{:S(2)}, u32[]{:S(2)}) %all-to-all-start.1) | async-done | bytes 31457312 | tf_op jit(solution)/shard_map/all_to_all | solution.py:35
  502.7 15.2 %convolution_convert_fusion = bf16[225,4096]{1,0:T(8,128)(2,1)} fusion(bf16[3840,225]{0,1:T(8,128)(2,1)} %reshape.47, bf16[3840,4096]{1,0:T(8,128)(2,1)} %bitcast.4), kind=kOutput, calls=%fused_computation | convolution fusion | flops 7078809600 | bytes 35028480 | tf_op jit(solution)/shard_map/dot_general | solution.py:32
  (2 shorter events, 0.0 us)
Async XLA Ops:
  6.5 53.4 %copy-start = (f32[60,480]{1,0:T(8,128)S(1)}, f32[60,480]{1,0:T(8,128)}, u32[]{:S(2)}) copy-start(f32[60,480]{1,0:T(8,128)} %param.4) | copy-start | bytes 345604
  53.3 449.5 %all-to-all-start.1 = ((bf16[16,240,4096]{2,1,0:T(8,128)(2,1)}), bf16[16,240,4096]{2,1,0:T(8,128)(2,1)}, u32[]{:S(2)}, u32[]{:S(2)}) async-start(bf16[16,240,4096]{2,1,0:T(8,128)(2,1)} %stack.5), calls=%async_computation.1 | async-start | bytes 62914560 | tf_op jit(solution)/shard_map/all_to_all | solution.py:35
  59.9 1.7 copy-start.1
  59.9 56.6 %all-gather.3.cloned.1.call-start = ((), (), s32[]{:S(2)}) async-start(), calls=%async_computation.2 | async-start | bytes 2138112 | tf_op jit(solution)/shard_map/all_gather | solution.py:30
Sparse Core Ops, SparseCore 0:
  63.1 53.2 all-gather.2
